TPU v7x, 32 devices: a whole 2x2x4 slice. The times are simulated.
32 devices in a mesh: grp: 2 (over y), tok: 8 (over z, x), head: 2 (over core).
Axes of the slice: x: 2, y: 2, z: 4, core: 2. Of those that a mesh axis runs over, the one named last changes fastest.
Arguments:
- events: bfloat16 [16384, 1024], P(('grp', 'tok')), parts along dimension 0, may hold values from -6 to 6
- uvqk_weight: bfloat16 [1024, 4, 1024], P(None, None, 'head'), may hold values from -0.1875 to 0.1875
- out_weight: bfloat16 [1024, 1024], P('head'), may hold values from -0.1875 to 0.1875
- segments: int32 [16, 1024], P(('grp', 'tok')), parts along dimension 0, may hold values from 0 to 7, never falling along the last dimension, each value on 1 to 512 neighbouring positions
Outputs:
- targets: bfloat16 [16384, 1024], P(('grp', 'tok'), 'head'), parts along dimension 0
There are 2 independent parts, one for each index of `grp`. A program takes and returns all parts, laid end to end along the dimension named above; an argument that names none is the same for every part. Nothing has to cross between parts.
Inputs may be any that keep to these rules, and one draw needn't show every extreme that they name: `segments`: in each row numbers never fall; every user 0 to 7 holds 1 to 512 consecutive rows of its owner, and some user holds exactly 512.
All inputs are finite; a program needn't handle non-finite values.
Results may differ from a plain program's by a relative error of at most 0.007.
Values may be sent and summed in bfloat16 or wider, within the bound.
A program may use at most 64 MiB of HBM per device.

v0:
```python
import jax
import jax.numpy as jnp
from jax import lax
from jax.sharding import PartitionSpec as P

HD = 128
USERS_OWN = 8
BLK = 128


def project(features, uvqk_weight):
    mixed_rows = jnp.einsum(
        "td,dkf->tkf", features, uvqk_weight, preferred_element_type=jnp.float32
    )
    return jax.nn.silu(mixed_rows).astype(jnp.bfloat16)


def positions(segments, user_count):
    user_ids = jnp.arange(user_count, dtype=jnp.int32)
    member = (segments[:, None] == user_ids[None, :]).astype(jnp.int32)
    counts = jnp.sum(member, axis=0)
    firsts = jnp.cumsum(counts) - counts
    first_row = jnp.sum(member * firsts[None, :], axis=1)
    return jnp.arange(segments.shape[0], dtype=jnp.int32) - first_row


def attend(uvqk_rows, segments):
    row_count = uvqk_rows.shape[0]
    heads_here = uvqk_rows.shape[2] // HD
    split_rows = uvqk_rows.reshape(row_count, 4, heads_here, HD)
    gate_rows = split_rows[:, 0]
    value_rows = split_rows[:, 1]
    query_rows = split_rows[:, 2]
    key_rows = split_rows[:, 3]
    blocks = positions(segments, USERS_OWN) // BLK
    qblock = min(512, row_count)
    block_count = row_count // qblock

    def one_block(block_index):
        begin_row = block_index * qblock
        query_part = lax.dynamic_slice_in_dim(query_rows, begin_row, qblock, 0)
        gate_part = lax.dynamic_slice_in_dim(gate_rows, begin_row, qblock, 0)
        seg_part = lax.dynamic_slice_in_dim(segments, begin_row, qblock, 0)
        blk_part = lax.dynamic_slice_in_dim(blocks, begin_row, qblock, 0)
        scores = jnp.einsum(
            "qhe,khe->hqk", query_part, key_rows, preferred_element_type=jnp.float32
        ) * HD ** (-0.5)
        allowed = (seg_part[:, None] == segments[None, :]) & (blocks[None, :] <= blk_part[:, None])
        weights = jnp.where(allowed[None], jax.nn.silu(scores), 0.0).astype(jnp.bfloat16)
        mixed_rows = jnp.einsum(
            "hqk,khe->qhe", weights, value_rows, preferred_element_type=jnp.float32
        )
        normed = mixed_rows * lax.rsqrt(
            jnp.mean(mixed_rows * mixed_rows, axis=-1, keepdims=True) + 1e-06
        )
        return (
            (normed * gate_part.astype(jnp.float32))
            .astype(jnp.bfloat16)
            .reshape(qblock, heads_here * HD)
        )

    outputs = lax.map(one_block, jnp.arange(block_count, dtype=jnp.int32))
    return outputs.reshape(row_count, heads_here * HD)


def per_device(events, uvqk_weight, out_weight, segments):
    owners = lax.axis_size("tok")
    row_count = events.shape[0]
    slot_rows = row_count // owners
    dim_model = events.shape[1]
    pair_count = lax.axis_size("head")
    half_rows = slot_rows // pair_count
    sliced = events.reshape(owners, pair_count, half_rows, dim_model)
    mine = lax.dynamic_index_in_dim(sliced, lax.axis_index("head"), 1, keepdims=False)
    received = lax.all_to_all(mine, "tok", split_axis=0, concat_axis=0, tiled=True)
    joined = lax.all_gather(received, "head", axis=1, tiled=True)
    uvqk_rows = project(joined.reshape(row_count, dim_model), uvqk_weight)
    attended = attend(uvqk_rows, segments[0])
    head_width = attended.shape[1]
    returned = lax.all_to_all(
        attended.reshape(owners, slot_rows, head_width),
        "tok",
        split_axis=0,
        concat_axis=0,
        tiled=True,
    )
    returned = returned.reshape(row_count, head_width)
    partial_value = jnp.dot(returned, out_weight, preferred_element_type=jnp.float32)
    branch = lax.psum_scatter(
        partial_value.astype(jnp.bfloat16), "head", scatter_dimension=1, tiled=True
    ).astype(jnp.float32)
    half_width = branch.shape[1]
    residual = lax.dynamic_slice_in_dim(events, lax.axis_index("head") * half_width, half_width, 1)
    return (residual.astype(jnp.float32) + branch).astype(jnp.bfloat16)


def solution(mesh):
    in_specs = (
        P(("grp", "tok"), None),
        P(None, None, "head"),
        P("head", None),
        P(("grp", "tok"), None),
    )
    out_specs = P(("grp", "tok"), "head")
    return jax.shard_map(
        per_device, mesh=mesh, in_specs=in_specs, out_specs=out_specs, check_vma=False
    )
```

profile of v0, /device:TPU:27, one launch (start us, length us, event | category | flops | bytes accessed | tf_op | source)
XLA Modules:
  0.0 135.8 jit_solution(5182719253599515043)
XLA Ops:
  6.5 1.4 %dynamic-slice_bitcast_fusion = bf16[8,64,1024]{2,1,0:T(8,128)(2,1)S(1)} fusion(bf16[8,2,64,1024]{3,2,1,0:T(8,128)(2,1)} %bitcast.41, s32[]{:T(128)S(6)} %select_n.24), kind=kLoop, calls=%fused_computation.21 | loop fusion | bytes 2097156 | tf_op jit(solution)/shard_map/jit(dynamic_index_in_dim)/squeeze | solution.py:74
  8.0 28.9 %all_to_all.10 = bf16[8,64,1024]{2,1,0:T(8,128)(2,1)} all-to-all(bf16[8,64,1024]{2,1,0:T(8,128)(2,1)S(1)} %dynamic-slice_bitcast_fusion), channel_id=1, replica_groups=mesh['grp'=2,'tok'=8,'head'=2] {'tok'}, dimensions={0} | all-to-all | bytes 2097152 | tf_op jit(solution)/shard_map/all_to_all | solution.py:75
  37.4 12.3 %all-gather.2.cloned.1.call-done = bf16[8,128,1024]{2,1,0:T(8,128)(2,1)} async-done(((bf16[8,64,1024]{2,1,0:T(8,128)(2,1)}), bf16[8,128,1024]{2,1,0:T(8,128)(2,1)}) %all-gather.2.cloned.1.call-update) | async-done | bytes 2097168 | tf_op jit(solution)/shard_map/all_gather | solution.py:76
  49.7 8.7 %multiply_convert_fusion.1 = bf16[1024,4,512]{0,2,1:T(8,128)(2,1)S(1)} fusion(bf16[1024,1024,1]{1,0,2:T(8,128)(2,1)} %bitcast.53, bf16[1024,4,512]{2,1,0:T(4,128)(2,1)} %param.7), kind=kOutput, calls=%fused_computation.14 | convolution fusion | flops 4305453056 | bytes 10485760 | tf_op jit(solution)/shard_map/td,dkf->tkf/dot_general | solution.py:12
  58.4 2.0 %slice_bitcast_fusion = (bf16[1024,4,128]{0,2,1:T(8,128)(2,1)}, bf16[1024,1,4,128]{0,3,2,1:T(8,128)(2,1)S(1)}, bf16[1024,4,128]{0,2,1:T(8,128)(2,1)}, bf16[1024,1,4,128]{0,3,2,1:T(8,128)(2,1)S(1)}) fusion(bf16[1024,4,4,128]{0,3,2,1:T(8,128)(2,1)S(1)} %bitcast.40), kind=kLoop, calls=%fused_computation.19 | loop fusion | bytes 8388608 | tf_op jit(solution)/shard_map/squeeze | solution.py:31
  60.4 1.3 copy.16
  61.7 1.3 copy.17
  63.0 19.9 %while.10 = (s32[]{:T(128)}, bf16[2,512,512]{2,1,0:T(8,128)(2,1)}, s32[2]{0:T(128)S(1)}, s32[1024]{0:T(1024)S(1)}, s32[1,1024]{1,0:T(1,128)S(1)}, /*index=5*/s32...) while((s32[]{:T(128)}, bf16[2,512,512]{2,1,0:T(8,128)(2,1)}, ...), condition=%wide.region_5.6_spmd, body=%wide.region_3.5_spmd.sunk | while | flops 1091569664 | bytes 8966863 | solution.py:62
  63.0 0.6 dynamic_slice.40
  64.4 0.5 compare_and_fusion.2
  64.9 5.8 %multiply_reduce_fusion.2 = (f32[512,4]{0,1:T(4,128)S(1)}, f32[512,4,128]{0,2,1:T(8,128)S(1)}) fusion(bf16[1024,4,128]{0,2,1:T(8,128)(2,1)} %get-tuple-element.185, pred[512,1024]{1,0:T(8,128)(4,1)S(1)} %compare_and_fusion.2, bf16[1024,4,128]{2,0,1:T(8,128)(2,1)} %get-tuple-element.184, bf16[1024,4,128]{2,0,1:T(8,128)(2,1)} %get-tuple-element.183, ...), kind=kOutput, calls=%fused_computation.6.clone.1 | convolution fusion | flops 1088944128 | bytes 4202500 | tf_op jit(solution)/shard_map/while/body/eval_jaxpr/hqk,khe->qhe/dot_general | solution.py:50
  70.7 1.2 multiply_convert_fusion.3
  71.9 0.2 copy.23
  72.1 0.8 constant_dynamic-update-slice_fusion.2
  73.0 0.6 dynamic_slice.40
  74.3 0.5 compare_and_fusion.2
  74.8 5.8 %multiply_reduce_fusion.2 = (f32[512,4]{0,1:T(4,128)S(1)}, f32[512,4,128]{0,2,1:T(8,128)S(1)}) fusion(bf16[1024,4,128]{0,2,1:T(8,128)(2,1)} %get-tuple-element.185, pred[512,1024]{1,0:T(8,128)(4,1)S(1)} %compare_and_fusion.2, bf16[1024,4,128]{2,0,1:T(8,128)(2,1)} %get-tuple-element.184, bf16[1024,4,128]{2,0,1:T(8,128)(2,1)} %get-tuple-element.183, ...), kind=kOutput, calls=%fused_computation.6.clone.1 | convolution fusion | flops 1088944128 | bytes 4202500 | tf_op jit(solution)/shard_map/while/body/eval_jaxpr/hqk,khe->qhe/dot_general | solution.py:50
  80.7 1.2 multiply_convert_fusion.3
  81.9 0.2 copy.23
  82.1 0.8 constant_dynamic-update-slice_fusion.2
  82.9 29.4 %all_to_all.11 = bf16[8,128,512]{2,1,0:T(8,128)(2,1)S(1)} all-to-all(bf16[8,128,512]{2,1,0:T(8,128)(2,1)} %bitcast.44), channel_id=1, replica_groups=mesh['grp'=2,'tok'=8,'head'=2] {'tok'}, dimensions={0} | all-to-all | bytes 2097152 | tf_op jit(solution)/shard_map/all_to_all | solution.py:80
  112.3 2.6 %convolution_convert_fusion = bf16[1024,1024]{1,0:T(8,128)(2,1)} fusion(bf16[1024,512]{1,0:T(8,128)(2,1)S(1)} %bitcast.45, bf16[512,1024]{1,0:T(8,128)(2,1)S(1)} %copy-done), kind=kOutput, calls=%fused_computation.18 | convolution fusion | flops 1074790400 | bytes 4194304 | tf_op jit(solution)/shard_map/dot_general | solution.py:88
  115.0 11.4 %reduce-scatter.2.cloned.1.call-done = bf16[1024,512]{1,0:T(8,128)(2,1)} async-done(((bf16[1024,1024]{1,0:T(8,128)(2,1)}), bf16[1024,512]{1,0:T(8,128)(2,1)}) %reduce-scatter.2.cloned.1.call-update) | async-done | bytes 1048592 | tf_op jit(solution)/shard_map/reduce_scatter | solution.py:89
  126.3 2.6 %add_convert_fusion = bf16[1024,512]{1,0:T(8,128)(2,1)} fusion(bf16[1024,512]{1,0:T(8,128)(2,1)} %reduce-scatter.2.cloned.1.call-done, bf16[1024,1024]{1,0:T(8,128)(2,1)S(1)} %copy-done.1, s32[]{:T(128)S(6)} %select_n.22), kind=kLoop, calls=%fused_computation.17 | loop fusion | flops 2097152 | bytes 3145732 | tf_op jit(solution)/shard_map/convert_element_type | solution.py:94
  (23 shorter events, 0.8 us)
Async XLA Ops:
  6.5 105.8 %copy-start = (bf16[512,1024]{1,0:T(8,128)(2,1)S(1)}, bf16[512,1024]{1,0:T(8,128)(2,1)}, u32[]{:S(2)}) copy-start(bf16[512,1024]{1,0:T(8,128)(2,1)} %param.8) | copy-start | bytes 3145732
  6.5 30.4 %copy-start.2 = (s32[1,1024]{1,0:T(1,128)S(1)}, s32[1,1024]{1,0:T(1,128)}, u32[]{:S(2)}) copy-start(s32[1,1024]{1,0:T(1,128)} %param.9) | copy-start | bytes 12292
  6.5 43.1 %all-gather.2.cloned.1.call-start = ((), (), s32[]{:S(2)}) async-start(), calls=%async_computation.3 | async-start | bytes 3145728 | tf_op jit(solution)/shard_map/all_gather | solution.py:76
  36.9 89.4 %reduce-scatter.2.cloned.1.call-start = ((), (), s32[]{:S(2)}) async-start(), calls=%async_computation.4 | async-start | bytes 3145728 | tf_op jit(solution)/shard_map/reduce_scatter | solution.py:89
  112.3 14.0 %copy-start.1 = (bf16[1024,1024]{1,0:T(8,128)(2,1)S(1)}, bf16[1024,1024]{1,0:T(8,128)(2,1)}, u32[]{:S(2)}) copy-start(bf16[1024,1024]{1,0:T(8,128)(2,1)} %param.6) | copy-start | bytes 6291460
Sparse Core Ops, SparseCore 0:
  37.0 12.5 all-gather.1
  115.1 11.2 reduce-scatter.1
where the time goes:
time: 137 us; the launch traced here: 136 us
  blocking collectives  58.3 us (43%)
  waiting for transfers between devices  23.7 us (17%)
  matrix products  22.9 us (17%)
  between operations  13.5 us (10%)
  local copies, waits for them, and re-layouts  9.68 us (7%)
  other arithmetic  6.43 us (5%)
    all_to_all x1, blocking collectives, per_device(): lax.all_to_all(attended.reshape(owners, slot_rows, head_width), 'tok', sp...  29.4 us
    all_to_all x1, blocking collectives, per_device(): lax.all_to_all(mine, 'tok', split_axis=0, concat_axis=0, tiled=True)  28.9 us
    all_gather x1, waiting for transfers between devices, per_device(): joined = lax.all_gather(received, 'head', axis=1, tiled=True)  12.3 us
    dot_general x2, matrix products, one_block(): jnp.einsum('hqk,khe->qhe', weights, value_rows, preferred_element_type=jn...  11.6 us
    reduce_scatter x1, waiting for transfers between devices, per_device(): lax.psum_scatter(partial_value.astype(jnp.bfloat16), 'head', scatter_dime...  11.4 us
    dot_general x1, matrix products, project(): jnp.einsum('td,dkf->tkf', features, uvqk_weight, preferred_element_type=j...  8.69 us
  transfers between devices with their start and end apart: 2, of which 2 were waited for; matrix products, arithmetic and copies ran while one was open for 0% of the time, Pallas kernels for 0%

commit v1 on v0

v1 whole, which is shorter than its diff:
```python
import functools

import jax
import jax.numpy as jnp
from jax import lax
from jax.experimental import pallas as pl
from jax.experimental.pallas import tpu as pltpu
from jax.sharding import PartitionSpec as P

HD = 128
USERS_OWN = 8
BLK = 128
MAXLEN = 512
MESH = pl.DeviceIdType.MESH


def half_silu(half):
    return half + half * jnp.tanh(half)


def kernel(
    owners, seg_ref, events, w_hbm, wo_hbm, out,
    xb, wv, wov, uvqk, lo_ref, hi_ref, own_part, prx, ptx, obuf,
    w_sem, wo_sem, loc_sem, in_send, in_recv, fwd_send, fwd_recv,
    pp_send, pp_recv, out_send, out_recv, ol_sem,
):
    grp, me, core = lax.axis_index("grp"), lax.axis_index("tok"), lax.axis_index("head")
    rows, dim = events.shape
    slot = rows // owners
    half = out.shape[1]
    width = wo_hbm.shape[0]
    heads = width // HD
    tiles = rows // BLK
    per_tile = BLK // slot
    mine = pl.ds(pl.multiple_of(core * half, half), half)
    theirs = pl.ds(pl.multiple_of((1 - core) * half, half), half)

    def peer(i):
        if owners & (owners - 1):
            return lax.rem(me + i, owners)
        total, bit = 0, 1
        while bit < owners:
            total = total + ((me // bit + i // bit) % 2) * bit
            bit *= 2
        return total

    def slot_rows(s):
        return pl.ds(pl.multiple_of(s * slot, slot), slot)

    def in_copy(s, d):
        return pltpu.make_async_remote_copy(
            src_ref=events.at[slot_rows(d), mine], dst_ref=xb.at[slot_rows(s), mine],
            send_sem=in_send.at[d], recv_sem=in_recv.at[s],
            device_id=(grp, d, core), device_id_type=MESH)

    def fwd_copy(s, cols):
        return pltpu.make_async_remote_copy(
            src_ref=xb.at[slot_rows(s), cols], dst_ref=xb.at[slot_rows(s), cols],
            send_sem=fwd_send.at[s], recv_sem=fwd_recv.at[s],
            device_id=(grp, me, 1 - core), device_id_type=MESH)

    def pp_copy(t):
        return pltpu.make_async_remote_copy(
            src_ref=ptx.at[pl.ds(t * BLK, BLK)], dst_ref=prx.at[pl.ds(t * BLK, BLK)],
            send_sem=pp_send.at[t], recv_sem=pp_recv.at[t],
            device_id=(grp, me, 1 - core), device_id_type=MESH)

    def out_copy(s, d):
        return pltpu.make_async_remote_copy(
            src_ref=obuf.at[slot_rows(d)], dst_ref=out.at[slot_rows(s)],
            send_sem=out_send.at[d], recv_sem=out_recv.at[s],
            device_id=(grp, d, core), device_id_type=MESH)

    out_local = pltpu.make_async_copy(obuf.at[slot_rows(me)], out.at[slot_rows(me)], ol_sem)
    x_local = pltpu.make_async_copy(events.at[slot_rows(me)], xb.at[slot_rows(me)], loc_sem)
    w_copy = pltpu.make_async_copy(w_hbm, wv, w_sem)
    wo_copy = pltpu.make_async_copy(wo_hbm, wov, wo_sem)

    barrier = pltpu.get_barrier_semaphore()

    @pl.loop(1, owners)
    def _(i):
        pl.semaphore_signal(barrier, inc=1, device_id=(grp, peer(i), core), device_id_type=MESH)

    pl.semaphore_signal(barrier, inc=1, device_id=(grp, me, 1 - core), device_id_type=MESH)
    x_local.start()
    w_copy.start()
    wo_copy.start()
    pl.semaphore_wait(barrier, owners)

    @pl.loop(1, owners)
    def _(i):
        d = peer(owners - i)
        in_copy(me, d).start()

    segr = seg_ref[...]
    seg_t = jnp.transpose(jnp.broadcast_to(segr, (BLK, rows)))
    row = lax.broadcasted_iota(jnp.int32, (rows, BLK), 0)
    starts = [
        jnp.sum((segr < u).astype(jnp.int32), axis=1, keepdims=True) for u in range(USERS_OWN + 1)
    ]
    first = jnp.zeros((rows, BLK), jnp.int32)
    end = jnp.zeros((rows, BLK), jnp.int32)
    for u in range(USERS_OWN):
        here = seg_t == u
        first = jnp.where(here, starts[u], first)
        end = jnp.where(here, starts[u + 1], end)
    blocks = lax.shift_right_logical(row - first, BLK.bit_length() - 1)
    lo_ref[...] = first
    hi_ref[...] = jnp.minimum(end, first + (blocks + 1) * BLK)

    def project(s):
        x = xb[slot_rows(s), :]
        for k in range(4):
            cols = slice(k * width, (k + 1) * width)
            v = jnp.dot(x, wv[:, cols], preferred_element_type=jnp.float32)
            uvqk[slot_rows(s), cols] = half_silu(v * 0.5).astype(jnp.bfloat16)

    x_local.wait()
    w_copy.wait()
    project(me)
    s1 = peer(1)
    in_copy(s1, s1).wait_recv()
    fwd_copy(s1, mine).start()

    @pl.loop(2, owners)
    def _(i):
        s, before = peer(i), peer(i - 1)
        in_copy(s, s).wait_recv()
        fwd_copy(s, mine).start()
        fwd_copy(before, theirs).wait_recv()
        project(before)

    last = peer(owners - 1)
    fwd_copy(last, theirs).wait_recv()
    project(last)
    wo_copy.wait()

    def finish(t):
        pp_copy(t).wait_recv()
        r = pl.ds(t * BLK, BLK)
        total = (
            xb[r, mine].astype(jnp.float32)
            + own_part[r, :].astype(jnp.float32)
            + prx[r, :].astype(jnp.float32)
        )
        obuf[r, :] = total.astype(jnp.bfloat16)
        for p in range(per_tile):
            s = t * per_tile + p

            @pl.when(s == me)
            def _():
                out_local.start()

            @pl.when(s != me)
            def _():
                out_copy(me, s).start()

    scale = 0.5 * HD ** (-0.5)
    reach = MAXLEN // BLK
    for t in range(tiles):
        a, b = max(0, t - reach), min(tiles, t + 2)
        r = slice(t * BLK, (t + 1) * BLK)
        keys = slice(a * BLK, b * BLK)
        span = (b - a) * BLK
        at = lax.broadcasted_iota(jnp.int32, (BLK, span), 1) + a * BLK
        lo = jnp.concatenate([lo_ref[r, :]] * (b - a), axis=1)
        hi = jnp.concatenate([hi_ref[r, :]] * (b - a), axis=1)
        allowed = (at >= lo) & (at < hi)
        columns = []
        for h in range(heads):
            def part(k):
                return slice(k * width + h * HD, k * width + (h + 1) * HD)

            scores = lax.dot_general(
                uvqk[r, part(2)], uvqk[keys, part(3)], (((1,), (1,)), ((), ())),
                preferred_element_type=jnp.float32)
            weights = jnp.where(allowed, half_silu(scores * scale), 0.0).astype(jnp.bfloat16)
            mixed = jnp.dot(weights, uvqk[keys, part(1)], preferred_element_type=jnp.float32)
            normed = mixed * lax.rsqrt(jnp.mean(mixed * mixed, axis=-1, keepdims=True) + 1e-06)
            columns.append((normed * uvqk[r, part(0)].astype(jnp.float32)).astype(jnp.bfloat16))
        att = jnp.concatenate(columns, axis=1)
        ptx[r, :] = jnp.dot(att, wov[:, theirs], preferred_element_type=jnp.float32).astype(jnp.bfloat16)
        pp_copy(t).start()
        own_part[r, :] = jnp.dot(att, wov[:, mine], preferred_element_type=jnp.float32).astype(jnp.bfloat16)
        if t:
            finish(t - 1)
    finish(tiles - 1)

    @pl.loop(1, owners)
    def _(i):
        s = peer(i)
        in_copy(me, s).wait_send()
        fwd_copy(s, mine).wait_send()
        out_copy(me, s).wait_send()
        out_copy(s, s).wait_recv()

    for t in range(tiles):
        pp_copy(t).wait_send()
    out_local.wait()


def per_device(events, uvqk_weight, out_weight, segments):
    owners = lax.axis_size("tok")
    rows, dim = events.shape
    width = uvqk_weight.shape[2]
    half = dim // lax.axis_size("head")
    tiles = rows // BLK
    w2 = uvqk_weight.reshape(dim, 4 * width)
    dma = pltpu.SemaphoreType.DMA
    hbm = pl.BlockSpec(memory_space=pl.ANY)
    bf = jnp.bfloat16
    return pl.pallas_call(
        functools.partial(kernel, owners),
        out_shape=jax.ShapeDtypeStruct((rows, half), bf),
        in_specs=[pl.BlockSpec(memory_space=pltpu.VMEM), hbm, hbm, hbm],
        out_specs=hbm,
        scratch_shapes=[
            pltpu.VMEM((rows, dim), bf),
            pltpu.VMEM((dim, 4 * width), bf),
            pltpu.VMEM((width, dim), bf),
            pltpu.VMEM((rows, 4 * width), bf),
            pltpu.VMEM((rows, BLK), jnp.int32),
            pltpu.VMEM((rows, BLK), jnp.int32),
            pltpu.VMEM((rows, half), bf),
            pltpu.VMEM((rows, half), bf),
            pltpu.VMEM((rows, half), bf),
            pltpu.VMEM((rows, half), bf),
            dma, dma, dma,
            dma((owners,)), dma((owners,)), dma((owners,)), dma((owners,)),
            dma((tiles,)), dma((tiles,)), dma((owners,)), dma((owners,)), dma,
        ],
        compiler_params=pltpu.CompilerParams(
            collective_id=0, has_side_effects=True, vmem_limit_bytes=48 * 2**20
        ),
    )(segments, events, w2, out_weight)


def solution(mesh):
    in_specs = (
        P(("grp", "tok"), None),
        P(None, None, "head"),
        P("head", None),
        P(("grp", "tok"), None),
    )
    return jax.shard_map(
        per_device, mesh=mesh, in_specs=in_specs, out_specs=P(("grp", "tok"), "head"), check_vma=False
    )
```

time: 137 us -> 69.3 us (0.51)
  Pallas kernels: 0 us -> 62.5 us
  blocking collectives: 58.3 us -> 0 us
  waiting for transfers between devices: 23.7 us -> 0 us
  matrix products: 22.9 us -> 0 us
  between operations: 13.5 us -> 0.02 us
  other arithmetic: 6.43 us -> 0 us
  local copies, waits for them, and re-layouts: 9.68 us -> 6.66 us
    pallas_call x0 -> x1, Pallas kernels: none -> 62.5 us  [per_device(): pl.pallas_call(functools.partial(kernel, owners), out_shape=jax.ShapeDtyp...]
    all_to_all x2 -> x0, blocking collectives: 58.3 us -> none  [the longest x1 29.4 us: per_device(): lax.all_to_all(attended.reshape(owners, slot_rows, head_width), 'tok', sp...]
    dot_general x4 -> x0, matrix products: 22.9 us -> none  [the longest x2 11.6 us: one_block(): jnp.einsum('hqk,khe->qhe', weights, value_rows, preferred_element_type=jn...]
    all_gather x1 -> x0, waiting for transfers between devices: 12.3 us -> none  [per_device(): joined = lax.all_gather(received, 'head', axis=1, tiled=True)]
    reduce_scatter x1 -> x0, waiting for transfers between devices: 11.4 us -> none  [per_device(): lax.psum_scatter(partial_value.astype(jnp.bfloat16), 'head', scatter_dime...]
    convert_element_type x3 -> x0, other arithmetic: 5.03 us -> none  [the longest x1 2.59 us: per_device(): return (residual.astype(jnp.float32) + branch).astype(jnp.bfloat16)]
    unnamed x8, local copies, waits for them, and re-layouts: 2.65 us -> 6.66 us
    squeeze x2 -> x0, local copies, waits for them, and re-layouts: 3.41 us -> none  [the longest x1 1.98 us: attend(): gate_rows = split_rows[:, 0]]
  transfers between devices with their start and end apart: 2 -> 0, of which waited for: 2 -> 0; matrix products, arithmetic and copies ran while one was open for 0% -> 0% of each run, Pallas kernels for 0% -> 0%
where the time goes in v1:
time: 69.3 us; the launch traced here: 69.1 us
  Pallas kernels  62.5 us (90%)
  local copies, waits for them, and re-layouts  6.66 us (10%)
    pallas_call x1, Pallas kernels, per_device(): pl.pallas_call(functools.partial(kernel, owners), out_shape=jax.ShapeDtyp...  62.5 us
    unnamed x8, local copies, waits for them, and re-layouts  6.66 us

profile of v1, /device:TPU:27, one launch (start us, length us, event | category | flops | bytes accessed | tf_op | source)
XLA Modules:
  0.0 69.1 jit_solution(16444465894150584156)
XLA Ops:
  0.0 0.0 copy-start
  0.0 0.0 copy-start.1
  0.0 0.0 copy-start.2
  0.0 5.7 %copy.5 = bf16[128,8,4,512]{3,1,2,0:T(8,128)(2,1)} copy(bf16[128,8,4,512]{3,2,1,0:T(4,128)(2,1)} %bitcast.3) | data formatting | bytes 8388608
  5.7 0.0 copy-done
  5.7 0.0 copy-done.1
  5.7 0.0 copy-done.2
  5.7 62.5 %shard_map.46 = bf16[1024,512]{1,0:T(8,128)(2,1)S(1)} custom-call(s32[1,1024]{1,0:T(1,128)S(1)} %copy-done.2, bf16[1024,1024]{1,0:T(8,128)(2,1)S(1)} %copy-done, bf16[1024,2048]{1,0:T(8,128)(2,1)} %bitcast.2, bf16[512,1024]{1,0:T(8,128)(2,1)S(1)} %copy-done.1), custom_call_target="tpu_custom_call" | custom-call | tf_op jit(solution)/shard_map/pallas_call | solution.py:213
  68.2 1.0 %copy.7 = bf16[1024,512]{1,0:T(8,128)(2,1)} copy(bf16[1024,512]{1,0:T(8,128)(2,1)S(1)} %shard_map.46) | data formatting | bytes 2097152
Async XLA Ops:
  0.0 5.7 %copy-start = (bf16[1024,1024]{1,0:T(8,128)(2,1)S(1)}, bf16[1024,1024]{1,0:T(8,128)(2,1)}, u32[]{:S(2)}) copy-start(bf16[1024,1024]{1,0:T(8,128)(2,1)} %events.1) | copy-start | bytes 6291460
  0.0 5.7 %copy-start.1 = (bf16[512,1024]{1,0:T(8,128)(2,1)S(1)}, bf16[512,1024]{1,0:T(8,128)(2,1)}, u32[]{:S(2)}) copy-start(bf16[512,1024]{1,0:T(8,128)(2,1)} %wo_hbm.1) | copy-start | bytes 3145732
  0.0 5.7 %copy-start.2 = (s32[1,1024]{1,0:T(1,128)S(1)}, s32[1,1024]{1,0:T(1,128)}, u32[]{:S(2)}) copy-start(s32[1,1024]{1,0:T(1,128)} %seg_ref.1) | copy-start | bytes 12292

commit v2 on v1

--- a/solution.py
+++ b/solution.py
@@ -19,9 +19,9 @@
 
 
 def kernel(
-    owners, seg_ref, events, w_hbm, wo_hbm, out,
-    xb, wv, wov, uvqk, lo_ref, hi_ref, own_part, prx, ptx, obuf,
-    w_sem, wo_sem, loc_sem, in_send, in_recv, fwd_send, fwd_recv,
+    owners, seg_hbm, events, w_hbm, wo_hbm, out,
+    seg_ref, xb, w3, wv, wov, uvqk, lo_ref, hi_ref, own_part, prx, ptx, obuf,
+    seg_sem, w_sem, wo_sem, loc_sem, in_send, in_recv, fwd_send, fwd_recv,
     pp_send, pp_recv, out_send, out_recv, ol_sem,
 ):
     grp, me, core = lax.axis_index("grp"), lax.axis_index("tok"), lax.axis_index("head")
@@ -47,15 +47,20 @@
     def slot_rows(s):
         return pl.ds(pl.multiple_of(s * slot, slot), slot)
 
+    def share(s, c):
+        if slot % 32:
+            return slot_rows(s), pl.ds(pl.multiple_of(c * half, half), half)
+        return pl.ds(pl.multiple_of(s * slot + c * (slot // 2), slot // 2), slot // 2), slice(None)
+
     def in_copy(s, d):
         return pltpu.make_async_remote_copy(
-            src_ref=events.at[slot_rows(d), mine], dst_ref=xb.at[slot_rows(s), mine],
+            src_ref=events.at[share(d, core)], dst_ref=xb.at[share(s, core)],
             send_sem=in_send.at[d], recv_sem=in_recv.at[s],
             device_id=(grp, d, core), device_id_type=MESH)
 
-    def fwd_copy(s, cols):
-        return pltpu.make_async_remote_copy(
-            src_ref=xb.at[slot_rows(s), cols], dst_ref=xb.at[slot_rows(s), cols],
+    def fwd_copy(s, c):
+        return pltpu.make_async_remote_copy(
+            src_ref=xb.at[share(s, c)], dst_ref=xb.at[share(s, c)],
             send_sem=fwd_send.at[s], recv_sem=fwd_recv.at[s],
             device_id=(grp, me, 1 - core), device_id_type=MESH)
 
@@ -73,7 +78,7 @@
 
     out_local = pltpu.make_async_copy(obuf.at[slot_rows(me)], out.at[slot_rows(me)], ol_sem)
     x_local = pltpu.make_async_copy(events.at[slot_rows(me)], xb.at[slot_rows(me)], loc_sem)
-    w_copy = pltpu.make_async_copy(w_hbm, wv, w_sem)
+    w_copy = pltpu.make_async_copy(w_hbm, w3, w_sem)
     wo_copy = pltpu.make_async_copy(wo_hbm, wov, wo_sem)
 
     barrier = pltpu.get_barrier_semaphore()
@@ -83,6 +88,8 @@
         pl.semaphore_signal(barrier, inc=1, device_id=(grp, peer(i), core), device_id_type=MESH)
 
     pl.semaphore_signal(barrier, inc=1, device_id=(grp, me, 1 - core), device_id_type=MESH)
+    seg_copy = pltpu.make_async_copy(seg_hbm, seg_ref, seg_sem)
+    seg_copy.start()
     x_local.start()
     w_copy.start()
     wo_copy.start()
@@ -90,9 +97,10 @@
 
     @pl.loop(1, owners)
     def _(i):
-        d = peer(owners - i)
+        d = peer(i)
         in_copy(me, d).start()
 
+    seg_copy.wait()
     segr = seg_ref[...]
     seg_t = jnp.transpose(jnp.broadcast_to(segr, (BLK, rows)))
     row = lax.broadcasted_iota(jnp.int32, (rows, BLK), 0)
@@ -116,26 +124,6 @@
             v = jnp.dot(x, wv[:, cols], preferred_element_type=jnp.float32)
             uvqk[slot_rows(s), cols] = half_silu(v * 0.5).astype(jnp.bfloat16)
 
-    x_local.wait()
-    w_copy.wait()
-    project(me)
-    s1 = peer(1)
-    in_copy(s1, s1).wait_recv()
-    fwd_copy(s1, mine).start()
-
-    @pl.loop(2, owners)
-    def _(i):
-        s, before = peer(i), peer(i - 1)
-        in_copy(s, s).wait_recv()
-        fwd_copy(s, mine).start()
-        fwd_copy(before, theirs).wait_recv()
-        project(before)
-
-    last = peer(owners - 1)
-    fwd_copy(last, theirs).wait_recv()
-    project(last)
-    wo_copy.wait()
-
     def finish(t):
         pp_copy(t).wait_recv()
         r = pl.ds(t * BLK, BLK)
@@ -158,7 +146,7 @@
 
     scale = 0.5 * HD ** (-0.5)
     reach = MAXLEN // BLK
-    for t in range(tiles):
+    def attend(t):
         a, b = max(0, t - reach), min(tiles, t + 2)
         r = slice(t * BLK, (t + 1) * BLK)
         keys = slice(a * BLK, b * BLK)
@@ -183,15 +171,75 @@
         ptx[r, :] = jnp.dot(att, wov[:, theirs], preferred_element_type=jnp.float32).astype(jnp.bfloat16)
         pp_copy(t).start()
         own_part[r, :] = jnp.dot(att, wov[:, mine], preferred_element_type=jnp.float32).astype(jnp.bfloat16)
-        if t:
-            finish(t - 1)
-    finish(tiles - 1)
+
+    def run(order):
+        for n, t in enumerate(order):
+            attend(t)
+            if n:
+                finish(order[n - 1])
+        finish(order[-1])
+
+    x_local.wait()
+    w_copy.wait()
+
+    @pl.loop(0, dim // BLK)
+    def _(i):
+        d = pl.ds(pl.multiple_of(i * BLK, BLK), BLK)
+        for k in range(4):
+            wv[d, k * width:(k + 1) * width] = w3[d, k, :]
+
+    project(me)
+    s1 = peer(1)
+    in_copy(s1, s1).wait_recv()
+    fwd_copy(s1, core).start()
+
+    def step(i):
+        s, before = peer(i), peer(i - 1)
+        in_copy(s, s).wait_recv()
+        fwd_copy(s, core).start()
+        fwd_copy(before, 1 - core).wait_recv()
+        project(before)
+
+    near = owners // 2
+    split = near > 1 and not owners & (owners - 1) and tiles >= 4
+    middle = tiles // 2
+    if split:
+        pl.loop(2, near)(step)
+        fwd_copy(peer(near - 1), 1 - core).wait_recv()
+        project(peer(near - 1))
+        wo_copy.wait()
+
+        @pl.when(me < near)
+        def _():
+            run(list(range(middle - 1)))
+
+        nxt = peer(near)
+        in_copy(nxt, nxt).wait_recv()
+        fwd_copy(nxt, core).start()
+        pl.loop(near + 1, owners)(step)
+    else:
+        pl.loop(2, owners)(step)
+    last = peer(owners - 1)
+    fwd_copy(last, 1 - core).wait_recv()
+    project(last)
+    if split:
+        @pl.when(me < near)
+        def _():
+            run(list(range(middle, tiles)) + [middle - 1])
+
+        @pl.when(me >= near)
+        def _():
+            run(list(range(tiles)))
+    else:
+        wo_copy.wait()
+        run(list(range(tiles)))
+
 
     @pl.loop(1, owners)
     def _(i):
         s = peer(i)
         in_copy(me, s).wait_send()
-        fwd_copy(s, mine).wait_send()
+        fwd_copy(s, core).wait_send()
         out_copy(me, s).wait_send()
         out_copy(s, s).wait_recv()
 
@@ -206,17 +254,18 @@
     width = uvqk_weight.shape[2]
     half = dim // lax.axis_size("head")
     tiles = rows // BLK
-    w2 = uvqk_weight.reshape(dim, 4 * width)
     dma = pltpu.SemaphoreType.DMA
     hbm = pl.BlockSpec(memory_space=pl.ANY)
     bf = jnp.bfloat16
     return pl.pallas_call(
         functools.partial(kernel, owners),
         out_shape=jax.ShapeDtypeStruct((rows, half), bf),
-        in_specs=[pl.BlockSpec(memory_space=pltpu.VMEM), hbm, hbm, hbm],
+        in_specs=[hbm] * 4,
         out_specs=hbm,
         scratch_shapes=[
+            pltpu.VMEM((1, rows), jnp.int32),
             pltpu.VMEM((rows, dim), bf),
+            pltpu.VMEM((dim, 4, width), bf),
             pltpu.VMEM((dim, 4 * width), bf),
             pltpu.VMEM((width, dim), bf),
             pltpu.VMEM((rows, 4 * width), bf),
@@ -226,14 +275,14 @@
             pltpu.VMEM((rows, half), bf),
             pltpu.VMEM((rows, half), bf),
             pltpu.VMEM((rows, half), bf),
-            dma, dma, dma,
+            dma, dma, dma, dma,
             dma((owners,)), dma((owners,)), dma((owners,)), dma((owners,)),
             dma((tiles,)), dma((tiles,)), dma((owners,)), dma((owners,)), dma,
         ],
         compiler_params=pltpu.CompilerParams(
-            collective_id=0, has_side_effects=True, vmem_limit_bytes=48 * 2**20
+            collective_id=0, has_side_effects=True, vmem_limit_bytes=61 * 2**20
         ),
-    )(segments, events, w2, out_weight)
+    )(segments, events, uvqk_weight, out_weight)
 
 
 def solution(mesh):

time: 69.3 us -> 59.6 us (0.86)
  Pallas kernels: 62.5 us -> 57.2 us
  local copies, waits for them, and re-layouts: 6.66 us -> 2.26 us
    pallas_call x1, Pallas kernels: 62.5 us -> 57.2 us  [per_device(): pl.pallas_call(functools.partial(kernel, owners), out_shape=jax.ShapeDtyp...]
    unnamed x8 -> x1, local copies, waits for them, and re-layouts: 6.66 us -> 2.26 us
where the time goes in v2:
time: 59.6 us; the launch traced here: 59.5 us
  Pallas kernels  57.2 us (96%)
  local copies, waits for them, and re-layouts  2.26 us (4%)
    pallas_call x1, Pallas kernels, per_device(): pl.pallas_call(functools.partial(kernel, owners), out_shape=jax.ShapeDtyp...  57.2 us
    unnamed x1, local copies, waits for them, and re-layouts  2.26 us

profile of v2, /device:TPU:27, one launch (start us, length us, event | category | flops | bytes accessed | tf_op | source)
XLA Modules:
  0.0 59.5 jit_solution(17372981633400300059)
XLA Ops:
  0.0 57.2 %shard_map.46 = bf16[1024,512]{1,0:T(8,128)(2,1)} custom-call(s32[1,1024]{1,0:T(1,128)} %seg_hbm.1, bf16[1024,1024]{1,0:T(8,128)(2,1)} %events.1, bf16[1024,4,512]{2,1,0:T(4,128)(2,1)} %w_hbm.1, bf16[512,1024]{1,0:T(8,128)(2,1)} %wo_hbm.1), custom_call_target="tpu_custom_call" | custom-call | tf_op jit(solution)/shard_map/pallas_call | solution.py:260
  57.2 2.3 %copy.6 = bf16[1024,512]{1,0:T(8,128)(2,1)} copy(bf16[1024,512]{1,0:T(8,128)(2,1)} %shard_map.46) | data formatting | bytes 2097152
